TPU v7x, 32 devices: a whole 2x2x4 slice. The times are simulated.
32 devices in a mesh: row: 4 (over y, x), col: 2 (over core), depth: 4 (over z).
Axes of the slice: x: 2, y: 2, z: 4, core: 2. Of those that a mesh axis runs over, the one named last changes fastest.
Arguments:
- x_vals: bfloat16 [4, 16, 4, 128, 128], P('row', ('col', 'depth')), may hold values from -2.5 to 2.5
- x_rows: int32 [4, 16, 4], P('row', ('col', 'depth')), may hold values from -1 to 3, as said below
- out_block: int32 [4, 2, 4], P('row', 'col', 'depth'), may hold values from 0 to 15, as said below
Outputs:
- product_blocks: bfloat16 [4, 2, 4, 128, 128], P('row', 'col', 'depth')
Inputs may be any that keep to these rules, and one draw needn't show every extreme that they name: `x_rows`: within one row group and block column the filled slots name distinct rows. In every row group, each run of 2 block columns that starts at a multiple of 2 has a column with all 4 slots filled. `out_block`: within one tile the 4 entries are distinct positions, and every tile lists position 15 among them.
All inputs are finite; a program needn't handle non-finite values.
Results may differ from a plain program's by a relative error of at most 0.001.
Values may be sent and summed in bfloat16 or wider, within the bound.
A program may use at most 128 MiB of HBM per device.

v0:
```python
import functools

import jax
import jax.numpy as jnp
from jax import lax
from jax.experimental import pallas as pl
from jax.experimental.pallas import tpu as pltpu
from jax.sharding import PartitionSpec as P

MESH = pl.DeviceIdType.MESH
CHUNKS = 4
VMEM_LIMIT = 55072 * 1024


def product(left, right):
    return lax.dot_general(
        left, right, (((1,), (1,)), ((), ())), preferred_element_type=jnp.float32
    )


def kernel(
    sizes, rows_hbm, pos_ref, x_ref, out_ref,
    rows_ref, raw, home, partner, pos_vmem, left, send_parts, recv_parts,
    local_sem, home_send, home_recv, partner_send, partner_recv,
    pos_send, pos_recv, sum_send, sum_recv,
):
    row_count, col_count, depth_count = sizes
    width, slots, size = x_ref.shape[1], x_ref.shape[2], x_ref.shape[3]
    chunks, group_rows, sub = home.shape[1:4]
    wide = home.shape[4]
    midpoint = col_count // 2
    row, col, depth = (lax.axis_index(name) for name in ("row", "col", "depth"))
    has_partner = col != midpoint

    def place(row_index, col_index, depth_index):
        return {"row": row_index, "col": col_index, "depth": depth_index}

    loads = [
        pltpu.make_async_copy(x_ref.at[0], raw, local_sem.at[0]),
        pltpu.make_async_copy(rows_hbm, rows_ref, local_sem.at[1]),
        pltpu.make_async_copy(pos_ref.at[0], pos_vmem.at[0], local_sem.at[2]),
    ]
    for copy in loads:
        copy.start()

    barrier = pltpu.get_barrier_semaphore()

    def greet(device):
        pl.semaphore_signal(barrier, inc=1, device_id=device, device_id_type=MESH)

    for step in range(1, col_count):
        greet(place(row, lax.rem(col + step, col_count), depth))
    for step in range(1, depth_count):
        greet(place(row, col, lax.rem(depth + step, depth_count)))

    @pl.when(has_partner)
    def _():
        source_row = lax.rem(row + col - midpoint + row_count, row_count)
        for step in range(col_count):
            greet(place(source_row, lax.rem(col + step, col_count), depth))

    for copy in loads:
        copy.wait()
    for column in range(width):
        for block_row in range(group_rows):
            slot = jnp.int32(0)
            found = jnp.int32(0)
            for index in range(slots):
                match = rows_ref[0, column, index] == block_row
                slot = jnp.where(match, index, slot)
                found = jnp.where(match, 1, found)
            block = raw[column, slot]
            block = jnp.where(found > 0, block, jnp.zeros_like(block))
            home[0, :, block_row, :, column * size:(column + 1) * size] = block.reshape(
                chunks, sub, size
            )

    pl.semaphore_wait(barrier, 2 * (col_count - 1) + depth_count - 1)

    def home_copy(step):
        return pltpu.make_async_remote_copy(
            src_ref=home.at[0],
            dst_ref=home.at[step],
            send_sem=home_send.at[step],
            recv_sem=home_recv.at[step],
            device_id=place(row, lax.rem(col + step, col_count), depth),
            device_id_type=MESH,
        )

    def partner_copy(step, chunk):
        target_col = lax.rem(col + step, col_count)
        target_row = lax.rem(row + midpoint - target_col + row_count, row_count)
        return pltpu.make_async_remote_copy(
            src_ref=home.at[0, chunk],
            dst_ref=partner[chunk].at[step],
            send_sem=partner_send.at[step, chunk],
            recv_sem=partner_recv.at[step, chunk],
            device_id=place(target_row, target_col, depth),
            device_id_type=MESH,
        )

    def pos_copy(step):
        return pltpu.make_async_remote_copy(
            src_ref=pos_vmem.at[0],
            dst_ref=pos_vmem.at[step],
            send_sem=pos_send.at[step],
            recv_sem=pos_recv.at[step],
            device_id=place(row, col, lax.rem(depth + step, depth_count)),
            device_id_type=MESH,
        )

    def sum_copy(step, chunk):
        columns = pl.ds(chunk * sub, sub)
        return pltpu.make_async_remote_copy(
            src_ref=send_parts.at[step, columns],
            dst_ref=recv_parts.at[step, columns],
            send_sem=sum_send.at[step, chunk],
            recv_sem=sum_recv.at[step, chunk],
            device_id=place(row, col, lax.rem(depth + step, depth_count)),
            device_id_type=MESH,
        )

    def sends_partner(step):
        return lax.rem(col + step, col_count) != midpoint

    for step in range(1, depth_count):
        pos_copy(step).start()
    for chunk in range(chunks):
        for step in range(col_count):
            pl.when(sends_partner(step))(lambda: partner_copy(step, chunk).start())
            if step and not chunk:
                home_copy(step).start()
    for step in range(1, depth_count):
        pos_copy(step).wait_recv()
    positions = [pos_vmem[step, 0, 0] for step in range(depth_count)]
    for step in range(1, col_count):
        home_copy(step).wait_recv()

    steps = list(range(1, depth_count)) + [0]
    for step in steps:
        left_row = lax.div(positions[(depth_count - step) % depth_count], group_rows)
        left[step] = jnp.concatenate(
            [home[index, :, left_row].reshape(size, wide) for index in range(col_count)], axis=1
        )

    def tile(read, chunk):
        columns = slice(chunk * sub, (chunk + 1) * sub)
        totals = []
        for step in steps:
            right_row = lax.rem(positions[(depth_count - step) % depth_count], group_rows)
            right = jnp.concatenate(
                [read(index, chunk, right_row) for index in range(col_count)], axis=1
            )
            totals.append(product(right, left[step]))
        for step, total in zip(steps, totals):
            send_parts[step, columns] = total
        for step in range(1, depth_count):
            sum_copy(step, chunk).start()

    @pl.when(has_partner)
    def _():
        for chunk in range(chunks):
            for step in range(col_count):
                partner_copy(step, chunk).wait_recv()
            tile(lambda index, part, block_row: partner[part][index, block_row], chunk)

    @pl.when(jnp.logical_not(has_partner))
    def _():
        for chunk in range(chunks):
            tile(lambda index, part, block_row: home[index, part, block_row], chunk)

    for chunk in range(chunks):
        columns = slice(chunk * sub, (chunk + 1) * sub)
        total = send_parts[0, columns]
        for step in range(1, depth_count):
            sum_copy(step, chunk).wait_recv()
            total = total + recv_parts[step, columns]
        send_parts[0, columns] = total
    out_ref[0, 0, 0] = send_parts[0].T.astype(out_ref.dtype)

    for step in range(1, col_count):
        home_copy(step).wait_send()
    for step in range(1, depth_count):
        pos_copy(step).wait_send()
    for chunk in range(chunks):
        for step in range(col_count):
            pl.when(sends_partner(step))(lambda: partner_copy(step, chunk).wait_send())
        for step in range(1, depth_count):
            sum_copy(step, chunk).wait_send()


def on_device(sizes, x_vals, x_rows, out_block):
    row_count, col_count, depth_count = sizes
    _, width, slots, size, _ = x_vals.shape
    group_rows = width * col_count * depth_count // row_count
    staged = (col_count, CHUNKS, group_rows, size // CHUNKS, width * size)
    dma = pltpu.SemaphoreType.DMA
    return pl.pallas_call(
        functools.partial(kernel, sizes),
        out_shape=jax.ShapeDtypeStruct(out_block.shape + (size, size), jnp.bfloat16),
        in_specs=[
            pl.BlockSpec(memory_space=pl.ANY),
            pl.BlockSpec(memory_space=pl.ANY),
            pl.BlockSpec(memory_space=pl.ANY),
        ],
        out_specs=pl.BlockSpec(memory_space=pltpu.VMEM),
        scratch_shapes=[
            pltpu.SMEM(x_rows.shape, jnp.int32),
            pltpu.VMEM((width, slots, size, size), x_vals.dtype),
            pltpu.VMEM(staged, x_vals.dtype),
            tuple(pltpu.VMEM(staged[:1] + staged[2:], x_vals.dtype) for _ in range(CHUNKS)),
            pltpu.VMEM((depth_count,) + out_block.shape[1:], jnp.int32),
            pltpu.VMEM((depth_count, size, col_count * width * size), x_vals.dtype),
            pltpu.VMEM((depth_count, size, size), jnp.float32),
            pltpu.VMEM((depth_count, size, size), jnp.float32),
            dma((3,)),
            dma((col_count,)),
            dma((col_count,)),
            dma((col_count, CHUNKS)),
            dma((col_count, CHUNKS)),
            dma((depth_count,)),
            dma((depth_count,)),
            dma((depth_count, CHUNKS)),
            dma((depth_count, CHUNKS)),
        ],
        compiler_params=pltpu.CompilerParams(
            collective_id=0, has_side_effects=True, vmem_limit_bytes=VMEM_LIMIT
        ),
    )(x_rows, out_block, x_vals)


def solution(mesh):
    sizes = tuple(mesh.shape[name] for name in ("row", "col", "depth"))
    in_specs = (
        P("row", ("col", "depth"), None, None, None),
        P("row", ("col", "depth"), None),
        P("row", "col", "depth"),
    )
    out_specs = P("row", "col", "depth", None, None)
    return jax.shard_map(
        functools.partial(on_device, sizes),
        mesh=mesh, in_specs=in_specs, out_specs=out_specs, check_vma=False,
    )
```

profile of v0, /device:TPU:0, one launch (start us, length us, event | category | flops | bytes accessed | tf_op | source)
XLA Modules:
  0.0 18.9 jit_solution(18034815031603380753)
XLA Ops:
  0.0 0.0 copy-start
  0.7 0.0 copy-done
  0.7 17.6 %shard_map.37 = bf16[1,1,1,128,128]{4,3,2,1,0:T(8,128)(2,1)S(1)} custom-call(s32[1,2,4]{2,1,0:T(2,128)S(1)} %copy-done, s32[1,1,1]{2,1,0:T(1,128)S(6)} %copy.5.pos_ref, bf16[1,2,4,128,128]{4,3,2,1,0:T(8,128)(2,1)} %x_ref.1), custom_call_target="tpu_custom_call" | custom-call | tf_op jit(solution)/shard_map/pallas_call | solution.py:198
  18.3 0.6 %copy.6 = bf16[1,1,1,128,128]{4,3,2,1,0:T(8,128)(2,1)} copy(bf16[1,1,1,128,128]{4,3,2,1,0:T(8,128)(2,1)S(1)} %shard_map.37) | data formatting | bytes 65536
Async XLA Ops:
  0.0 0.7 %copy-start = (s32[1,2,4]{2,1,0:T(2,128)S(1)}, s32[1,2,4]{2,1,0:T(2,128)}, u32[]{:S(2)}) copy-start(s32[1,2,4]{2,1,0:T(2,128)} %rows_hbm.1) | copy-start | bytes 100
where the time goes:
time: 19 us; the launch traced here: 18.9 us
  Pallas kernels  17.6 us (93%)
  between operations  0.68 us (4%)
  local copies, waits for them, and re-layouts  0.63 us (3%)
    pallas_call x1, Pallas kernels, on_device(): pl.pallas_call(functools.partial(kernel, sizes), out_shape=jax.ShapeDtype...  17.6 us
    unnamed x3, local copies, waits for them, and re-layouts  0.63 us

commit v1 on v0

--- a/solution.py
+++ b/solution.py
@@ -61,6 +61,7 @@
 
     for copy in loads:
         copy.wait()
+    places = []
     for column in range(width):
         for block_row in range(group_rows):
             slot = jnp.int32(0)
@@ -69,11 +70,7 @@
                 match = rows_ref[0, column, index] == block_row
                 slot = jnp.where(match, index, slot)
                 found = jnp.where(match, 1, found)
-            block = raw[column, slot]
-            block = jnp.where(found > 0, block, jnp.zeros_like(block))
-            home[0, :, block_row, :, column * size:(column + 1) * size] = block.reshape(
-                chunks, sub, size
-            )
+            places.append((column, block_row, slot, found))
 
     pl.semaphore_wait(barrier, 2 * (col_count - 1) + depth_count - 1)
 
@@ -126,10 +123,17 @@
     for step in range(1, depth_count):
         pos_copy(step).start()
     for chunk in range(chunks):
+        lines = slice(chunk * sub, (chunk + 1) * sub)
+        for column, block_row, slot, found in places:
+            block = raw[column, slot, lines]
+            home[0, chunk, block_row, :, column * size:(column + 1) * size] = jnp.where(
+                found > 0, block, jnp.zeros_like(block)
+            )
         for step in range(col_count):
             pl.when(sends_partner(step))(lambda: partner_copy(step, chunk).start())
-            if step and not chunk:
-                home_copy(step).start()
+    for step in range(1, col_count):
+        home_copy(step).start()
+
     for step in range(1, depth_count):
         pos_copy(step).wait_recv()
     positions = [pos_vmem[step, 0, 0] for step in range(depth_count)]

time: 19 us -> 19 us (level)
  no operation moved by 1% of the time
where the time goes in v1:
time: 19 us; the launch traced here: 18.9 us
  Pallas kernels  17.6 us (93%)
  between operations  0.68 us (4%)
  local copies, waits for them, and re-layouts  0.63 us (3%)
    pallas_call x1, Pallas kernels, on_device(): pl.pallas_call(functools.partial(kernel, sizes), out_shape=jax.ShapeDtype...  17.6 us
    unnamed x3, local copies, waits for them, and re-layouts  0.63 us

profile of v1, /device:TPU:0, one launch (start us, length us, event | category | flops | bytes accessed | tf_op | source)
XLA Modules:
  0.0 18.9 jit_solution(10271492233438233613)
XLA Ops:
  0.0 0.0 copy-start
  0.7 0.0 copy-done
  0.7 17.6 %shard_map.37 = bf16[1,1,1,128,128]{4,3,2,1,0:T(8,128)(2,1)S(1)} custom-call(s32[1,2,4]{2,1,0:T(2,128)S(1)} %copy-done, s32[1,1,1]{2,1,0:T(1,128)S(6)} %copy.5.pos_ref, bf16[1,2,4,128,128]{4,3,2,1,0:T(8,128)(2,1)} %x_ref.1), custom_call_target="tpu_custom_call" | custom-call | tf_op jit(solution)/shard_map/pallas_call | solution.py:202
  18.3 0.6 %copy.6 = bf16[1,1,1,128,128]{4,3,2,1,0:T(8,128)(2,1)} copy(bf16[1,1,1,128,128]{4,3,2,1,0:T(8,128)(2,1)S(1)} %shard_map.37) | data formatting | bytes 65536
Async XLA Ops:
  0.0 0.7 %copy-start = (s32[1,2,4]{2,1,0:T(2,128)S(1)}, s32[1,2,4]{2,1,0:T(2,128)}, u32[]{:S(2)}) copy-start(s32[1,2,4]{2,1,0:T(2,128)} %rows_hbm.1) | copy-start | bytes 100

commit v2 on v1

--- a/solution.py
+++ b/solution.py
@@ -8,7 +8,7 @@
 from jax.sharding import PartitionSpec as P
 
 MESH = pl.DeviceIdType.MESH
-CHUNKS = 4
+CHUNKS = 2
 VMEM_LIMIT = 55072 * 1024
 
 

time: 19 us -> 19 us (level)
  no operation moved by 1% of the time
where the time goes in v2:
time: 19 us; the launch traced here: 18.9 us
  Pallas kernels  17.6 us (93%)
  between operations  0.68 us (4%)
  local copies, waits for them, and re-layouts  0.63 us (3%)
    pallas_call x1, Pallas kernels, on_device(): pl.pallas_call(functools.partial(kernel, sizes), out_shape=jax.ShapeDtype...  17.6 us
    unnamed x3, local copies, waits for them, and re-layouts  0.63 us

profile of v2, /device:TPU:0, one launch (start us, length us, event | category | flops | bytes accessed | tf_op | source)
XLA Modules:
  0.0 18.9 jit_solution(4041438782910016825)
XLA Ops:
  0.0 0.0 copy-start
  0.7 0.0 copy-done
  0.7 17.6 %shard_map.37 = bf16[1,1,1,128,128]{4,3,2,1,0:T(8,128)(2,1)S(1)} custom-call(s32[1,2,4]{2,1,0:T(2,128)S(1)} %copy-done, s32[1,1,1]{2,1,0:T(1,128)S(6)} %copy.5.pos_ref, bf16[1,2,4,128,128]{4,3,2,1,0:T(8,128)(2,1)} %x_ref.1), custom_call_target="tpu_custom_call" | custom-call | tf_op jit(solution)/shard_map/pallas_call | solution.py:202
  18.3 0.6 %copy.6 = bf16[1,1,1,128,128]{4,3,2,1,0:T(8,128)(2,1)} copy(bf16[1,1,1,128,128]{4,3,2,1,0:T(8,128)(2,1)S(1)} %shard_map.37) | data formatting | bytes 65536
Async XLA Ops:
  0.0 0.7 %copy-start = (s32[1,2,4]{2,1,0:T(2,128)S(1)}, s32[1,2,4]{2,1,0:T(2,128)}, u32[]{:S(2)}) copy-start(s32[1,2,4]{2,1,0:T(2,128)} %rows_hbm.1) | copy-start | bytes 100
